TPU v7x, 256 devices: a whole 4x4x8 slice. The times are simulated.
256 devices in a mesh: snap: 2 (over z_hi), row: 8 (over z_lo, core), col: 16 (over x, y).
Axes of the slice: x: 4, y: 4, z: 8 (z_hi: 2, z_lo: 4; z = z_hi * 4 + z_lo), core: 2. Of those that a mesh axis runs over, the one named last changes fastest.
Arguments:
- states: float32 [4096, 240], P(('snap', 'row', 'col')), may hold values from -8 to 8, as said below
- derivatives: float32 [4096, 240], P(('snap', 'row', 'col')), may hold values from -6 to 6
- tile_map: int32 [2048, 2], P(('snap', 'row', 'col')), may hold values from -1 to 113, as said below
Outputs:
- gram_tiles: float32 [2048, 256, 256], P(('snap', 'row', 'col'))
- rhs_blocks: float32 [128, 256, 240], P(('row', 'col'), None, 'snap')
Inputs may be any that keep to these rules, and one draw needn't show every extreme that they name: `states`: states are real coordinates of snapshots. `tile_map`: each entry is a pair a <= b of column tiles, or (-1, -1) for an empty slot; no pair appears twice. Each device's 8 slots hold its live pairs first, then empty ones; each device has at least 2 live slots and some device has all 8 live.
All inputs are finite; a program needn't handle non-finite values.
Results may differ from a plain program's by a relative error of at most 0.0003.
Values sent between devices are 32-bit elements; how exact they have to be, the bound alone decides.
A program may use at most 128 MiB of HBM per device.

v0:
```python
import jax
import jax.numpy as jnp
from jax import lax
from jax.sharding import PartitionSpec as P

TW = 256
CTILES = 114


precise_mode = lax.Precision.HIGHEST


def doubled_states(states):
    unit_column = jnp.ones((states.shape[0], 1), states.dtype)
    extended = jnp.concatenate([states, unit_column], 1)
    return jnp.concatenate([extended, extended], 1)


def feature_tile(doubled, tile_index, tile_width):
    block_width = doubled.shape[1] // 2
    feature_count = block_width * ((block_width + 1) // 2)
    columns = tile_index * tile_width + jnp.arange(tile_width, dtype=jnp.int32)
    valid = columns < feature_count
    safe_columns = jnp.where(valid, columns, 0)
    shift_part = safe_columns // block_width
    state_part = safe_columns % block_width
    left_values = jnp.take(doubled, state_part, axis=1)
    right_values = jnp.take(doubled, state_part + shift_part, axis=1)
    return jnp.where(valid[None, :], left_values * right_values, jnp.zeros_like(left_values))


def inner_product(left_block, right_block):
    return lax.dot_general(
        left_block,
        right_block,
        (((0,), (0,)), ((), ())),
        precision=precise_mode,
        preferred_element_type=jnp.float32,
    )


def build_tiles(doubled, slot_pairs, inv_snaps):
    slot_count = slot_pairs.shape[0]

    def advance(slot_index, gram_tiles):
        first_tile = slot_pairs[slot_index, 0]
        second_tile = slot_pairs[slot_index, 1]

        def compute(unused):
            left_block = feature_tile(doubled, jnp.maximum(first_tile, 0), TW)
            right_block = feature_tile(doubled, jnp.maximum(second_tile, 0), TW)
            return inner_product(left_block, right_block) * inv_snaps

        def skipped(unused):
            return jnp.zeros((TW, TW), jnp.float32)

        gram_tile = lax.cond(first_tile >= 0, compute, skipped, 0)
        return lax.dynamic_update_slice_in_dim(gram_tiles, gram_tile[None], slot_index, 0)

    initial = jnp.zeros((slot_count, TW, TW), jnp.float32)
    return lax.fori_loop(0, slot_count, advance, initial)


def local(states, derivatives, tile_map):
    panel_states, panel_derivs = (
        lax.all_gather(states, ("row", "col"), axis=0, tiled=True),
        lax.all_gather(derivatives, ("row", "col"), axis=0, tiled=True),
    )
    panel_rows = panel_states.shape[0]
    inv_snaps = 1.0 / (panel_rows * lax.axis_size("snap"))
    rhs_tile = lax.axis_index(("row", "col")) % CTILES
    slot_pairs = lax.all_gather(tile_map, "snap", axis=0, tiled=True)
    doubled = doubled_states(panel_states)
    gram_terms = build_tiles(doubled, slot_pairs, inv_snaps)
    rhs_term = inner_product(feature_tile(doubled, rhs_tile, TW), panel_derivs)[None] * inv_snaps
    gram_tiles, rhs_blocks = (
        lax.psum_scatter(gram_terms, "snap", scatter_dimension=0, tiled=True),
        lax.psum_scatter(rhs_term, "snap", scatter_dimension=2, tiled=True),
    )
    return (gram_tiles, rhs_blocks)


def solution(mesh):
    placed = (
        P(("snap", "row", "col"), None),
        P(("snap", "row", "col"), None),
        P(("snap", "row", "col"), None),
    )
    return jax.shard_map(
        local,
        mesh=mesh,
        in_specs=placed,
        out_specs=(P(("snap", "row", "col"), None, None), P(("row", "col"), None, "snap")),
        check_vma=False,
    )
```

profile of v0, /device:TPU:1, one launch (start us, length us, event | category | flops | bytes accessed | tf_op | source)
XLA Modules:
  0.0 1242.0 jit_solution(15178000415425257696)
XLA Ops:
  8.7 9.6 all-gather
  18.5 299.7 %all-gather.4.cloned.1.call-done = f32[2048,240]{1,0:T(8,128)} async-done(((f32[16,240]{1,0:T(8,128)}), f32[2048,240]{1,0:T(8,128)}) %all-gather.4.cloned.1.call-update) | async-done | bytes 1966096 | tf_op jit(solution)/shard_map/all_gather | solution.py:66
  318.2 1.9 copy.8
  320.2 2.3 pad_maximum_fusion
  322.5 4.5 gather_fusion.5
  327.0 5.7 gather_fusion.4
  332.8 291.4 %all-gather.6.cloned.1.call-done = f32[2048,240]{1,0:T(8,128)} async-done(((f32[16,240]{1,0:T(8,128)}), f32[2048,240]{1,0:T(8,128)}) %all-gather.6.cloned.1.call-update) | async-done | bytes 1966096 | tf_op jit(solution)/shard_map/all_gather | solution.py:67
  624.2 6.7 fusion.48
  631.1 206.9 %while.13 = (s32[]{:T(128)}, f32[16,256,256]{2,1,0:T(8,128)}, s32[16,2]{0,1:T(2,128)S(1)}, f32[2048,482]{0,1:T(8,128)}, s32[]{:T(128)}, /*index=5*/s32[]{:T(128)}) while((s32[]{:T(128)}, f32[16,256,256]{2,1,0:T(8,128)}, s32[16,2]{0,1:T(2,128)S(1)}, f32[2048,482]{0,1:T(8,128)}, s32[]{:T(128)}, /*index=5*/s32[]{:T(128)}) %tuple.52), condition=%wide.region_3.5_spmd, body=%wide.region_0.4_spmd.sunk | while | flops 1614903296 | bytes 25984728 | solution.py:61
  632.2 29.3 %conditional.2 = (f32[1,256,256]{2,1,0:T(8,128)S(1)}) conditional(s32[]{:T(128)} %convert_element_type.8, () %tuple.50, (s32[]{:T(128)}, f32[2048,482]{0,1:T(8,128)}, s32[16,2]{0,1:T(2,128)S(1)}, s32[]{:T(128)}) %tuple.51), branch_computations={%region_1.1_spmd, %region_2.3_spmd} | conditional | flops 1614903296 | bytes 25459792 | solution.py:57
  633.5 4.5 gather_fusion.3
  638.1 5.7 gather_fusion.2
  644.4 5.8 gather_fusion.1
  650.2 5.7 gather_fusion
  656.0 5.6 fusion.16
  663.5 29.3 %conditional.2 = (f32[1,256,256]{2,1,0:T(8,128)S(1)}) conditional(s32[]{:T(128)} %convert_element_type.8, () %tuple.50, (s32[]{:T(128)}, f32[2048,482]{0,1:T(8,128)}, s32[16,2]{0,1:T(2,128)S(1)}, s32[]{:T(128)}) %tuple.51), branch_computations={%region_1.1_spmd, %region_2.3_spmd} | conditional | flops 1614903296 | bytes 25459792 | solution.py:57
  664.8 4.5 gather_fusion.3
  669.3 5.7 gather_fusion.2
  675.7 5.8 gather_fusion.1
  681.4 5.7 gather_fusion
  687.2 5.6 fusion.16
  694.7 29.3 %conditional.2 = (f32[1,256,256]{2,1,0:T(8,128)S(1)}) conditional(s32[]{:T(128)} %convert_element_type.8, () %tuple.50, (s32[]{:T(128)}, f32[2048,482]{0,1:T(8,128)}, s32[16,2]{0,1:T(2,128)S(1)}, s32[]{:T(128)}) %tuple.51), branch_computations={%region_1.1_spmd, %region_2.3_spmd} | conditional | flops 1614903296 | bytes 25459792 | solution.py:57
  696.0 4.5 gather_fusion.3
  700.5 5.7 gather_fusion.2
  706.9 5.8 gather_fusion.1
  712.6 5.7 gather_fusion
  718.4 5.6 fusion.16
  733.7 0.8 constant_dynamic-update-slice_fusion.2
  735.7 29.3 %conditional.2 = (f32[1,256,256]{2,1,0:T(8,128)S(1)}) conditional(s32[]{:T(128)} %convert_element_type.8, () %tuple.50, (s32[]{:T(128)}, f32[2048,482]{0,1:T(8,128)}, s32[16,2]{0,1:T(2,128)S(1)}, s32[]{:T(128)}) %tuple.51), branch_computations={%region_1.1_spmd, %region_2.3_spmd} | conditional | flops 1614903296 | bytes 25459792 | solution.py:57
  737.0 4.5 gather_fusion.3
  741.5 5.7 gather_fusion.2
  747.9 5.8 gather_fusion.1
  753.6 5.7 gather_fusion
  759.4 5.6 fusion.16
  766.9 29.3 %conditional.2 = (f32[1,256,256]{2,1,0:T(8,128)S(1)}) conditional(s32[]{:T(128)} %convert_element_type.8, () %tuple.50, (s32[]{:T(128)}, f32[2048,482]{0,1:T(8,128)}, s32[16,2]{0,1:T(2,128)S(1)}, s32[]{:T(128)}) %tuple.51), branch_computations={%region_1.1_spmd, %region_2.3_spmd} | conditional | flops 1614903296 | bytes 25459792 | solution.py:57
  768.2 4.5 gather_fusion.3
  772.7 5.7 gather_fusion.2
  779.1 5.8 gather_fusion.1
  784.9 5.7 gather_fusion
  790.6 5.6 fusion.16
  798.1 29.3 %conditional.2 = (f32[1,256,256]{2,1,0:T(8,128)S(1)}) conditional(s32[]{:T(128)} %convert_element_type.8, () %tuple.50, (s32[]{:T(128)}, f32[2048,482]{0,1:T(8,128)}, s32[16,2]{0,1:T(2,128)S(1)}, s32[]{:T(128)}) %tuple.51), branch_computations={%region_1.1_spmd, %region_2.3_spmd} | conditional | flops 1614903296 | bytes 25459792 | solution.py:57
  799.4 4.5 gather_fusion.3
  804.0 5.7 gather_fusion.2
  810.3 5.8 gather_fusion.1
  816.1 5.7 gather_fusion
  821.9 5.6 fusion.16
  827.4 0.8 constant_dynamic-update-slice_fusion.2
  838.0 397.5 %reduce-scatter.3.cloned.1.call-done = f32[8,256,256]{2,1,0:T(8,128)} async-done(((f32[16,256,256]{2,1,0:T(8,128)}), f32[8,256,256]{2,1,0:T(8,128)}) %reduce-scatter.3.cloned.1.call-update) | async-done | bytes 2097168 | tf_op jit(solution)/shard_map/reduce_scatter | solution.py:77
  (128 shorter events, 26.3 us)
Async XLA Ops:
  7.2 311.1 %all-gather.4.cloned.1.call-start = ((), (), s32[]{:S(2)}) async-start(), calls=%async_computation.2 | async-start | bytes 2113536 | tf_op jit(solution)/shard_map/all_gather | solution.py:66
  7.9 616.3 %all-gather.6.cloned.1.call-start = ((), (), s32[]{:S(2)}) async-start(), calls=%async_computation.4 | async-start | bytes 2113536 | tf_op jit(solution)/shard_map/all_gather | solution.py:67
  8.6 829.3 %reduce-scatter.5.cloned.1.call-start = ((), (), s32[]{:S(2)}) async-start(), calls=%async_computation.5 | async-start | bytes 368640 | tf_op jit(solution)/shard_map/reduce_scatter | solution.py:78
  630.8 604.6 %reduce-scatter.3.cloned.1.call-start = ((), (), s32[]{:S(2)}) async-start(), calls=%async_computation.3 | async-start | bytes 6291456 | tf_op jit(solution)/shard_map/reduce_scatter | solution.py:77
Sparse Core Ops, SparseCore 0:
  9.8 308.3 all-gather.3
  320.1 304.0 all-gather.5
  630.9 22.9 reduce-scatter.4
  838.1 397.3 reduce-scatter.2
where the time goes:
time: 1240 us
  waiting for transfers between devices  990 us (80%)
  local copies, waits for them, and re-layouts  164 us (13%)
  matrix products  40.1 us (3%)
  loops' own time  17.5 us (1%)
  between operations  13.8 us (1%)
    reduce_scatter x1, waiting for transfers between devices, local(): lax.psum_scatter(gram_terms, 'snap', scatter_dimension=0, tiled=True)  397 us
    all_gather x1, waiting for transfers between devices, local(): lax.all_gather(states, ('row', 'col'), axis=0, tiled=True)  300 us
    all_gather x1, waiting for transfers between devices, local(): lax.all_gather(derivatives, ('row', 'col'), axis=0, tiled=True)  291 us
    gather x13, local copies, waits for them, and re-layouts, feature_tile(): left_values = jnp.take(doubled, state_part, axis=1)  74.4 us
    gather x13, local copies, waits for them, and re-layouts, feature_tile(): right_values = jnp.take(doubled, state_part + shift_part, axis=1)  66.2 us
    dot_general x7, matrix products, inner_product(): lax.dot_general(left_block, right_block, (((0,), (0,)), ((), ())), precis...  40.1 us
  transfers between devices with their start and end apart: 4, of which 3 were waited for; matrix products, arithmetic and copies ran while one was open for 16% of the time, Pallas kernels for 0%

commit v1 on v0

v1 whole, which is shorter than its diff:
```python
import functools

import jax
import jax.numpy as jnp
from jax import lax
from jax.experimental import pallas as pl
from jax.experimental.pallas import tpu as pltpu
from jax.sharding import PartitionSpec as P

TW = 256
CTILES = 114
LANES = 128
MESH = pl.DeviceIdType.MESH
NT = (((1,), (1,)), ((), ()))
NN = (((1,), (0,)), ((), ()))
HIGH = lax.Precision.HIGH


def ring_slots(nz):
    up = {d: 2 * d - 1 for d in range(1, nz // 2 + 1)}
    down = {d: 2 * d for d in range(1, (nz + 1) // 2)}
    return up, down


def tile_place(tile, width):
    column = tile * TW
    shift = lax.div(column, width)
    first = column - shift * width
    second = first + shift
    second = jnp.where(second >= width, second - width, second)
    return column, first, second


def tile_masks(column, first, width, features):
    rows = lax.broadcasted_iota(jnp.int32, (TW, LANES), 0)
    return rows >= width - first, rows >= 2 * width - first, rows + column < features


def feature_part(feat, plane, first, second, masks):
    wrap_one, wrap_two, valid = masks
    left = feat[plane, pl.ds(first, TW), :]
    right = jnp.where(wrap_one, feat[plane, pl.ds(second + 1, TW), :], feat[plane, pl.ds(second, TW), :])
    last = jnp.where(wrap_two[TW - 16 :], feat[plane, pl.ds(second + 2 + TW - 16, 16), :], right[TW - 16 :])
    product = left * jnp.concatenate([right[: TW - 16], last], 0)
    tail = jnp.where(valid[TW - 32 :], product[TW - 32 :], 0.0)
    return jnp.concatenate([product[: TW - 32], tail], 0)


def kernel(sizes, map_ref, states_ref, derivs_ref, gram_ref, rhs_ref, own, halves, land, column, derivs, feat, sems):
    nzh, nzl, ncol, block, states, features = sizes
    nz = nzh * nzl
    width = states + 1
    half = states // nzh
    per_slot = 2 * ncol * block // LANES
    up_slot, down_slot = ring_slots(nz)
    zh, row, col = lax.axis_index("snap"), lax.axis_index("row"), lax.axis_index("col")
    core = lax.rem(row, 2)
    z = zh * nzl + lax.div(row, 2)
    inv_snaps = 1.0 / (nz * 2 * ncol * block)

    def device(z_to, core_to, col_to):
        return {"snap": lax.div(z_to, nzl), "row": lax.rem(z_to, nzl) * 2 + core_to, "col": col_to}

    def along_z(e):
        return device(lax.rem(z + e + nz, nz), core, col)

    def in_plane(k):
        return device(z, core, lax.rem(col + k, ncol))

    sibling = device(z, 1 - core, col)

    def copy(src, dst, kind, index, to):
        send, recv = sems[kind]
        return pltpu.make_async_remote_copy(
            src_ref=src, dst_ref=dst, send_sem=send.at[index], recv_sem=recv.at[index], device_id=to, device_id_type=MESH
        )

    barrier = pltpu.get_barrier_semaphore()

    def greet(to):
        pl.semaphore_signal(barrier, inc=1, device_id=to, device_id_type=MESH)

    greet(sibling)
    lax.fori_loop(1, nz, lambda e, c: (greet(along_z(e)), c)[1], 0)
    lax.fori_loop(1, ncol, lambda k, c: (greet(in_plane(k)), c)[1], 0)

    own[...] = jnp.ones(own.shape, jnp.float32)
    own[:, :states] = states_ref[...]
    for h in range(nzh):
        halves[h] = jnp.zeros((block, LANES), jnp.float32)
        halves[h, :, :half] = derivs_ref[:, h * half : (h + 1) * half]
    land[0, 0, col] = own[...]
    column[0] = halves[zh]

    pl.semaphore_wait(barrier, 1 + (nz - 1) + (ncol - 1))

    def plane_copy(k):
        return copy(own, land.at[0, 0, col], "plane", k, in_plane(k))

    lax.fori_loop(1, ncol, lambda k, c: (plane_copy(k).start(), c)[1], 0)

    def column_copy(e):
        slot = up_slot[e] if e in up_slot else down_slot[nz - e]
        z_to = lax.rem(z + e, nz)
        return copy(halves.at[lax.div(z_to, nzl)], column.at[slot], "column", slot, along_z(e))

    for e in range(1, nz):
        column_copy(e).start()

    def up_copy(d):
        return copy(land.at[up_slot[d - 1] if d > 1 else 0, 0], land.at[up_slot[d], 0], "ring", up_slot[d], along_z(1))

    def down_copy(d):
        return copy(land.at[down_slot[d - 1] if d > 1 else 0, 0], land.at[down_slot[d], 0], "ring", down_slot[d], along_z(-1))

    def sibling_copy(slot):
        return copy(land.at[slot, 0], land.at[slot, 1], "sibling", slot, sibling)

    def spread_copy(k):
        return copy(column, derivs.at[0, :, col], "spread", k, in_plane(k))

    def across_copy():
        return copy(derivs.at[0], derivs.at[1], "across", 0, sibling)

    def ring_copies(d):
        return [c(d) for c, slots in ((up_copy, up_slot), (down_copy, down_slot)) if d in slots]

    def slots_at(d):
        return [s[d] for s in (up_slot, down_slot) if d in s]

    def transpose(slots):
        def one(n, carry):
            slot, part = slots[0] + lax.div(n, per_slot), lax.rem(n, per_slot)
            plane = slots[0] * per_slot + n
            per_core = per_slot // 2
            blocks = LANES // block
            which = pl.ds(lax.rem(part, per_core) * blocks, blocks)
            tile = land[slot, lax.div(part, per_core), which].reshape(LANES, 2 * LANES)
            turned = jnp.concatenate([tile[:, :LANES].T, tile[:, LANES:].T], 0)[:width]
            feat[plane, :width] = turned
            feat[plane, width : 2 * width] = turned
            feat[plane, 2 * width : 2 * width + 24] = turned[:24]
            return carry

        lax.fori_loop(0, len(slots) * per_slot, one, 0)

    def tile_value(tile, planes):
        at, first, second = tile_place(tile, width)
        masks = tile_masks(at, first, width, features)
        return jnp.concatenate([feature_part(feat, plane, first, second, masks) for plane in planes], 1)

    def gram(slots, first_time, last_time):
        planes = [s * per_slot + i for s in slots for i in range(per_slot)]

        def one(p, carry):
            a, b = map_ref[p, 0], map_ref[p, 1]
            term = lax.dot_general(
                tile_value(jnp.maximum(a, 0), planes),
                tile_value(jnp.maximum(b, 0), planes),
                NT,
                precision=HIGH,
                preferred_element_type=jnp.float32,
            )
            total = term if first_time else gram_ref[p] + term
            if last_time:
                total = jnp.where(a >= 0, total * inv_snaps, 0.0)
            gram_ref[p] = total
            return carry

        lax.fori_loop(0, gram_ref.shape[0], one, 0)

    far = nz // 2
    lax.fori_loop(1, ncol, lambda k, c: (plane_copy(k).wait_recv(), c)[1], 0)
    for c in ring_copies(1):
        c.start()
    sibling_copy(0).start()
    for slot in range(1, nz):
        copy(halves.at[0], column.at[slot], "column", slot, sibling).wait_recv()
    derivs[0, :, col] = column[...]
    lax.fori_loop(1, ncol, lambda k, c: (spread_copy(k).start(), c)[1], 0)
    sibling_copy(0).wait_recv()
    transpose([0])
    gram([0], True, False)
    ready = []
    for d in range(1, far + 1):
        for c in ring_copies(d):
            c.wait_recv()
        for slot in slots_at(d):
            sibling_copy(slot).start()
        if d < far:
            for c in ring_copies(d + 1):
                c.start()
        if d == far - 1:
            lax.fori_loop(1, ncol, lambda k, c: (spread_copy(k).wait_recv(), c)[1], 0)
            across_copy().start()
        for slot in slots_at(d):
            sibling_copy(slot).wait_recv()
        transpose(slots_at(d))
        gram(slots_at(d), False, d == far)

    across_copy().wait_recv()
    rhs_tile = lax.rem(row * ncol + col, CTILES)
    planes = range(nz * per_slot)
    halves_of = [derivs[c, s].reshape(ncol * block, LANES) for s in range(nz) for c in range(2)]
    total = lax.dot_general(
        tile_value(rhs_tile, planes), jnp.concatenate(halves_of, 0), NN, precision=HIGH, preferred_element_type=jnp.float32
    )
    rhs_ref[0] = total[:, :half] * inv_snaps

    lax.fori_loop(1, ncol, lambda k, c: (plane_copy(k).wait_send(), c)[1], 0)
    lax.fori_loop(1, ncol, lambda k, c: (spread_copy(k).wait_send(), c)[1], 0)
    for e in range(1, nz):
        column_copy(e).wait_send()
    for d in range(1, far + 1):
        for c in ring_copies(d):
            c.wait_send()
    for slot in range(nz):
        sibling_copy(slot).wait_send()
    across_copy().wait_send()


KINDS = ("plane", "column", "ring", "sibling", "spread", "across")


def entry(sizes, *refs):
    refs, flat = refs[: -2 * len(KINDS)], refs[-2 * len(KINDS) :]
    kernel(sizes, *refs, {k: flat[2 * i : 2 * i + 2] for i, k in enumerate(KINDS)})


def local(nzh, nzl, ncol, states, derivatives, tile_map):
    block, width = states.shape
    nz = nzh * nzl
    planes = nz * 2 * ncol * block // LANES
    features = (width + 1) * ((width + 2) // 2)
    slots = tile_map.shape[0]
    counts = {"plane": ncol, "column": nz, "ring": nz, "sibling": nz, "spread": ncol, "across": 1}
    return pl.pallas_call(
        functools.partial(entry, (nzh, nzl, ncol, block, width, features)),
        out_shape=(
            jax.ShapeDtypeStruct((slots, TW, TW), jnp.float32),
            jax.ShapeDtypeStruct((1, TW, width // nzh), jnp.float32),
        ),
        in_specs=[
            pl.BlockSpec(memory_space=pltpu.SMEM),
            pl.BlockSpec(memory_space=pltpu.VMEM),
            pl.BlockSpec(memory_space=pltpu.VMEM),
        ],
        out_specs=[pl.BlockSpec(memory_space=pltpu.VMEM)] * 2,
        scratch_shapes=[
            pltpu.VMEM((block, 2 * LANES), jnp.float32),
            pltpu.VMEM((nzh, block, LANES), jnp.float32),
            pltpu.VMEM((nz, 2, ncol, block, 2 * LANES), jnp.float32),
            pltpu.VMEM((nz, block, LANES), jnp.float32),
            pltpu.VMEM((2, nz, ncol, block, LANES), jnp.float32),
            pltpu.VMEM((planes, 2 * (width + 1) + 24, LANES), jnp.float32),
        ]
        + [pltpu.SemaphoreType.DMA((counts[k],)) for k in KINDS for _ in range(2)],
        compiler_params=pltpu.CompilerParams(collective_id=0, has_side_effects=True, vmem_limit_bytes=56 * 2**20),
    )(tile_map, states, derivatives)


def solution(mesh):
    nzh, rows, ncol = mesh.shape["snap"], mesh.shape["row"], mesh.shape["col"]
    placed = P(("snap", "row", "col"), None)
    return jax.shard_map(
        functools.partial(local, nzh, rows // 2, ncol),
        mesh=mesh,
        in_specs=(placed, placed, placed),
        out_specs=(P(("snap", "row", "col"), None, None), P(("row", "col"), None, "snap")),
        check_vma=False,
    )
```

time: 1240 us -> 73.3 us (0.06)
  waiting for transfers between devices: 990 us -> 0 us
  local copies, waits for them, and re-layouts: 164 us -> 6.04 us
  Pallas kernels: 0 us -> 66.4 us
  matrix products: 40.1 us -> 0 us
  loops' own time: 17.5 us -> 0 us
  between operations: 13.8 us -> 0.64 us
    all_gather x2 -> x0, waiting for transfers between devices: 591 us -> none  [the longest x1 300 us: local(): lax.all_gather(states, ('row', 'col'), axis=0, tiled=True)]
    reduce_scatter x2 -> x0, waiting for transfers between devices: 398 us -> none  [the longest x1 397 us: local(): lax.psum_scatter(gram_terms, 'snap', scatter_dimension=0, tiled=True)]
    gather x26 -> x0, local copies, waits for them, and re-layouts: 141 us -> none  [the longest x13 74.4 us: feature_tile(): left_values = jnp.take(doubled, state_part, axis=1)]
    pallas_call x0 -> x1, Pallas kernels: none -> 66.4 us  [local(): pl.pallas_call(functools.partial(entry, (nzh, nzl, ncol, block, width, fe...]
    dot_general x7 -> x0, matrix products: 40.1 us -> none  [inner_product(): lax.dot_general(left_block, right_block, (((0,), (0,)), ((), ())), precis...]
    another operation x17 -> x0, loops' own time: 17.5 us -> none  [the longest x1 9.47 us: build_tiles(): return lax.fori_loop(0, slot_count, advance, initial)]
  transfers between devices with their start and end apart: 4 -> 0, of which waited for: 3 -> 0; matrix products, arithmetic and copies ran while one was open for 16% -> 0% of each run, Pallas kernels for 0% -> 0%
where the time goes in v1:
time: 73.3 us; the launch traced here: 73.1 us
  Pallas kernels  66.4 us (91%)
  local copies, waits for them, and re-layouts  6.04 us (8%)
    pallas_call x1, Pallas kernels, local(): pl.pallas_call(functools.partial(entry, (nzh, nzl, ncol, block, width, fe...  66.4 us
    unnamed x2, local copies, waits for them, and re-layouts  4.39 us
    pallas_call x1, local copies, waits for them, and re-layouts, local(): pl.pallas_call(functools.partial(entry, (nzh, nzl, ncol, block, width, fe...  1.65 us

profile of v1, /device:TPU:1, one launch (start us, length us, event | category | flops | bytes accessed | tf_op | source)
XLA Modules:
  0.0 73.1 jit_solution(5477216800949298422)
XLA Ops:
  0.6 1.3 %copy.5.refs_0_ = s32[8,2]{1,0:T(8,128)} copy(s32[8,2]{0,1:T(2,128)} %param.5) | data formatting | bytes 128 | tf_op args[2]
  2.0 66.4 %shard_map.50 = (f32[8,256,256]{2,1,0:T(8,128)}, f32[1,256,120]{2,1,0:T(8,128)}) custom-call(s32[8,2]{1,0:T(8,128)} %copy.5.refs_0_, f32[16,240]{1,0:T(8,128)} %refs_1_.1, f32[16,240]{1,0:T(8,128)} %refs_2_.1), custom_call_target="tpu_custom_call" | custom-call | tf_op jit(solution)/shard_map/pallas_call | solution.py:237
  68.4 1.7 %copy.6 = f32[1,256,120]{1,2,0:T(8,128)} copy(f32[1,256,120]{2,1,0:T(8,128)} %get-tuple-element.3) | data formatting | bytes 245760 | tf_op jit(solution)/shard_map/pallas_call | solution.py:237
  70.0 3.0 %copy.8 = f32[8,256,256]{2,1,0:T(8,128)} copy(f32[8,256,256]{2,1,0:T(8,128)} %get-tuple-element.6) | data formatting | bytes 4194304

commit v2 on v1

--- a/solution.py
+++ b/solution.py
@@ -10,6 +10,9 @@
 TW = 256
 CTILES = 114
 LANES = 128
+GROUP = 16
+LEAD = GROUP - 1
+COPIES = 536
 MESH = pl.DeviceIdType.MESH
 NT = (((1,), (1,)), ((), ()))
 NN = (((1,), (0,)), ((), ()))
@@ -28,30 +31,59 @@
     first = column - shift * width
     second = first + shift
     second = jnp.where(second >= width, second - width, second)
-    return column, first, second
-
-
-def tile_masks(column, first, width, features):
-    rows = lax.broadcasted_iota(jnp.int32, (TW, LANES), 0)
-    return rows >= width - first, rows >= 2 * width - first, rows + column < features
-
-
-def feature_part(feat, plane, first, second, masks):
-    wrap_one, wrap_two, valid = masks
-    left = feat[plane, pl.ds(first, TW), :]
-    right = jnp.where(wrap_one, feat[plane, pl.ds(second + 1, TW), :], feat[plane, pl.ds(second, TW), :])
-    last = jnp.where(wrap_two[TW - 16 :], feat[plane, pl.ds(second + 2 + TW - 16, 16), :], right[TW - 16 :])
-    product = left * jnp.concatenate([right[: TW - 16], last], 0)
-    tail = jnp.where(valid[TW - 32 :], product[TW - 32 :], 0.0)
-    return jnp.concatenate([product[: TW - 32], tail], 0)
-
-
-def kernel(sizes, map_ref, states_ref, derivs_ref, gram_ref, rhs_ref, own, halves, land, column, derivs, feat, sems):
+    turn = lax.rem(first + GROUP - 1, GROUP)
+    wrap = lax.div(width - first + turn, GROUP)
+    return turn, wrap, first - turn + LEAD, second - turn + LEAD
+
+
+def feature_part(feat, plane, place):
+    turn, wrap, left, right = place
+    rows = lax.broadcasted_iota(jnp.int32, (GROUP, LANES), 0)
+
+    def read(start, size):
+        return feat[plane, pl.ds(start, size), :]
+
+    head_left = jnp.where(rows >= turn, read(left, GROUP), read(left + TW, GROUP))
+    tail_right = jnp.where(rows >= GROUP * wrap - GROUP + 1, read(right + TW + 2, GROUP), read(right + TW + 1, GROUP))
+    head_right = jnp.where(rows >= turn, read(right, GROUP), tail_right)
+    body_left = read(left + GROUP, TW - GROUP)
+    body_right = [read(right + GROUP * g + jnp.where(g >= wrap, 1, 0), GROUP) for g in range(1, TW // GROUP)]
+    return jnp.concatenate([head_left * head_right, body_left * jnp.concatenate(body_right, 0)], 0)
+
+
+def turn_rows(turned, value, turn):
+    for h in range(value.shape[1] // LANES):
+        part = value[:, h * LANES : (h + 1) * LANES]
+        turned[h, :TW] = part
+        turned[h, TW:] = part[:GROUP]
+    return jnp.concatenate([turned[h, pl.ds(turn, TW), :] for h in range(value.shape[1] // LANES)], 1)
+
+
+def pair_places(map_ref, p, width):
+    return [tile_place(jnp.maximum(map_ref[q, p], 0), width) for q in range(2)]
+
+
+def finish(width, features, inv_snaps, map_ref, turned_ref, rhs_in_ref, gram_ref, rhs_ref, turned):
+    p = pl.program_id(0)
+    (a, *_), (b, *_) = pair_places(map_ref, p, width)
+    total = pltpu.roll(turn_rows(turned, turned_ref[0], a), lax.rem(TW - b, TW), 1)
+    row_at = lax.broadcasted_iota(jnp.int32, (TW, TW), 0) + map_ref[0, p] * TW
+    col_at = lax.broadcasted_iota(jnp.int32, (TW, TW), 1) + map_ref[1, p] * TW
+    live = (map_ref[0, p] >= 0) & (row_at < features) & (col_at < features)
+    gram_ref[0] = jnp.where(live, total * inv_snaps, 0.0)
+
+    @pl.when(p == 0)
+    def _():
+        rhs_ref[...] = rhs_in_ref[...]
+
+
+def kernel(sizes, map_ref, states_ref, derivs_ref, gram_ref, rhs_ref, own, halves, plane_rows, land, column, derivs, feat, turned, sems):
     nzh, nzl, ncol, block, states, features = sizes
     nz = nzh * nzl
     width = states + 1
     half = states // nzh
-    per_slot = 2 * ncol * block // LANES
+    per_core = ncol * block // LANES
+    per_slot = 2 * per_core
     up_slot, down_slot = ring_slots(nz)
     zh, row, col = lax.axis_index("snap"), lax.axis_index("row"), lax.axis_index("col")
     core = lax.rem(row, 2)
@@ -89,13 +121,13 @@
     for h in range(nzh):
         halves[h] = jnp.zeros((block, LANES), jnp.float32)
         halves[h, :, :half] = derivs_ref[:, h * half : (h + 1) * half]
-    land[0, 0, col] = own[...]
+    plane_rows[col] = own[...]
     column[0] = halves[zh]
 
     pl.semaphore_wait(barrier, 1 + (nz - 1) + (ncol - 1))
 
     def plane_copy(k):
-        return copy(own, land.at[0, 0, col], "plane", k, in_plane(k))
+        return copy(own, plane_rows.at[col], "plane", k, in_plane(k))
 
     lax.fori_loop(1, ncol, lambda k, c: (plane_copy(k).start(), c)[1], 0)
 
@@ -128,49 +160,44 @@
     def slots_at(d):
         return [s[d] for s in (up_slot, down_slot) if d in s]
 
-    def transpose(slots):
+    def turn_plane():
+        blocks = LANES // block
+        for n in range(per_core):
+            tile = plane_rows[n * blocks : (n + 1) * blocks].reshape(LANES, 2 * LANES)
+            land[0, 0, n] = jnp.concatenate([tile[:, :LANES].T, tile[:, LANES:].T], 0)
+
+    def unfold(slots):
         def one(n, carry):
             slot, part = slots[0] + lax.div(n, per_slot), lax.rem(n, per_slot)
+            rows = land[slot, lax.div(part, per_core), lax.rem(part, per_core)][:width]
             plane = slots[0] * per_slot + n
-            per_core = per_slot // 2
-            blocks = LANES // block
-            which = pl.ds(lax.rem(part, per_core) * blocks, blocks)
-            tile = land[slot, lax.div(part, per_core), which].reshape(LANES, 2 * LANES)
-            turned = jnp.concatenate([tile[:, :LANES].T, tile[:, LANES:].T], 0)[:width]
-            feat[plane, :width] = turned
-            feat[plane, width : 2 * width] = turned
-            feat[plane, 2 * width : 2 * width + 24] = turned[:24]
+            feat[plane, :LEAD] = rows[width - LEAD :]
+            feat[plane, LEAD : LEAD + width] = rows
+            feat[plane, LEAD + width : LEAD + 2 * width] = rows
+            feat[plane, LEAD + 2 * width :] = rows[: COPIES - LEAD - 2 * width]
             return carry
 
         lax.fori_loop(0, len(slots) * per_slot, one, 0)
 
-    def tile_value(tile, planes):
-        at, first, second = tile_place(tile, width)
-        masks = tile_masks(at, first, width, features)
-        return jnp.concatenate([feature_part(feat, plane, first, second, masks) for plane in planes], 1)
-
-    def gram(slots, first_time, last_time):
+    def tile_value(place, planes):
+        return jnp.concatenate([feature_part(feat, plane, place) for plane in planes], 1)
+
+    def gram(slots, first_time):
         planes = [s * per_slot + i for s in slots for i in range(per_slot)]
 
         def one(p, carry):
-            a, b = map_ref[p, 0], map_ref[p, 1]
+            a, b = pair_places(map_ref, p, width)
             term = lax.dot_general(
-                tile_value(jnp.maximum(a, 0), planes),
-                tile_value(jnp.maximum(b, 0), planes),
-                NT,
-                precision=HIGH,
-                preferred_element_type=jnp.float32,
+                tile_value(a, planes), tile_value(b, planes), NT, precision=HIGH, preferred_element_type=jnp.float32
             )
-            total = term if first_time else gram_ref[p] + term
-            if last_time:
-                total = jnp.where(a >= 0, total * inv_snaps, 0.0)
-            gram_ref[p] = total
+            gram_ref[p] = term if first_time else gram_ref[p] + term
             return carry
 
-        lax.fori_loop(0, gram_ref.shape[0], one, 0)
+        lax.fori_loop(0, gram_ref.shape[0], one, 0, unroll=2)
 
     far = nz // 2
     lax.fori_loop(1, ncol, lambda k, c: (plane_copy(k).wait_recv(), c)[1], 0)
+    turn_plane()
     for c in ring_copies(1):
         c.start()
     sibling_copy(0).start()
@@ -179,8 +206,8 @@
     derivs[0, :, col] = column[...]
     lax.fori_loop(1, ncol, lambda k, c: (spread_copy(k).start(), c)[1], 0)
     sibling_copy(0).wait_recv()
-    transpose([0])
-    gram([0], True, False)
+    unfold([0])
+    gram([0], True)
     ready = []
     for d in range(1, far + 1):
         for c in ring_copies(d):
@@ -195,17 +222,22 @@
             across_copy().start()
         for slot in slots_at(d):
             sibling_copy(slot).wait_recv()
-        transpose(slots_at(d))
-        gram(slots_at(d), False, d == far)
+        unfold(slots_at(d))
+        gram(slots_at(d), False)
 
     across_copy().wait_recv()
     rhs_tile = lax.rem(row * ncol + col, CTILES)
+    place = tile_place(rhs_tile, width)
     planes = range(nz * per_slot)
-    halves_of = [derivs[c, s].reshape(ncol * block, LANES) for s in range(nz) for c in range(2)]
+    parts = [derivs[c, s].reshape(ncol * block, LANES) for s in range(nz) for c in range(2)]
     total = lax.dot_general(
-        tile_value(rhs_tile, planes), jnp.concatenate(halves_of, 0), NN, precision=HIGH, preferred_element_type=jnp.float32
+        tile_value(place, planes), jnp.concatenate(parts, 0), NN, precision=HIGH, preferred_element_type=jnp.float32
     )
-    rhs_ref[0] = total[:, :half] * inv_snaps
+    total = turn_rows(turned, total, place[0])
+    row_at = lax.broadcasted_iota(jnp.int32, total.shape, 0) + rhs_tile * TW
+    total = jnp.where(row_at < features, total * inv_snaps, 0.0)
+    turned_rhs = jnp.concatenate([total[:LANES].T, total[LANES:].T], 1)
+    rhs_ref[0] = turned_rhs[:half]
 
     lax.fori_loop(1, ncol, lambda k, c: (plane_copy(k).wait_send(), c)[1], 0)
     lax.fori_loop(1, ncol, lambda k, c: (spread_copy(k).wait_send(), c)[1], 0)
@@ -234,11 +266,11 @@
     features = (width + 1) * ((width + 2) // 2)
     slots = tile_map.shape[0]
     counts = {"plane": ncol, "column": nz, "ring": nz, "sibling": nz, "spread": ncol, "across": 1}
-    return pl.pallas_call(
+    gram_tiles, rhs = pl.pallas_call(
         functools.partial(entry, (nzh, nzl, ncol, block, width, features)),
         out_shape=(
             jax.ShapeDtypeStruct((slots, TW, TW), jnp.float32),
-            jax.ShapeDtypeStruct((1, TW, width // nzh), jnp.float32),
+            jax.ShapeDtypeStruct((1, width // nzh, TW), jnp.float32),
         ),
         in_specs=[
             pl.BlockSpec(memory_space=pltpu.SMEM),
@@ -249,14 +281,30 @@
         scratch_shapes=[
             pltpu.VMEM((block, 2 * LANES), jnp.float32),
             pltpu.VMEM((nzh, block, LANES), jnp.float32),
-            pltpu.VMEM((nz, 2, ncol, block, 2 * LANES), jnp.float32),
+            pltpu.VMEM((ncol, block, 2 * LANES), jnp.float32),
+            pltpu.VMEM((nz, 2, ncol * block // LANES, 2 * LANES, LANES), jnp.float32),
             pltpu.VMEM((nz, block, LANES), jnp.float32),
             pltpu.VMEM((2, nz, ncol, block, LANES), jnp.float32),
-            pltpu.VMEM((planes, 2 * (width + 1) + 24, LANES), jnp.float32),
+            pltpu.VMEM((planes, COPIES, LANES), jnp.float32),
+            pltpu.VMEM((2, TW + GROUP, LANES), jnp.float32),
         ]
         + [pltpu.SemaphoreType.DMA((counts[k],)) for k in KINDS for _ in range(2)],
-        compiler_params=pltpu.CompilerParams(collective_id=0, has_side_effects=True, vmem_limit_bytes=56 * 2**20),
-    )(tile_map, states, derivatives)
+        compiler_params=pltpu.CompilerParams(collective_id=0, has_side_effects=True, vmem_limit_bytes=40 * 2**20),
+    )(tile_map.T, states, derivatives)
+    tile = pl.BlockSpec((1, TW, TW), lambda p: (p, 0, 0))
+    side = pl.BlockSpec((1, width // nzh, TW), lambda p: (0, 0, 0))
+    gram_tiles, rhs = pl.pallas_call(
+        functools.partial(finish, width + 1, features, 1.0 / (nz * 2 * ncol * block)),
+        grid=(slots,),
+        out_shape=(
+            jax.ShapeDtypeStruct((slots, TW, TW), jnp.float32),
+            jax.ShapeDtypeStruct((1, width // nzh, TW), jnp.float32),
+        ),
+        in_specs=[pl.BlockSpec(memory_space=pltpu.SMEM), tile, side],
+        out_specs=[tile, side],
+        scratch_shapes=[pltpu.VMEM((2, TW + GROUP, LANES), jnp.float32)],
+    )(tile_map.T, gram_tiles, rhs)
+    return gram_tiles, rhs.transpose(0, 2, 1)
 
 
 def solution(mesh):

time: 73.3 us -> 66.3 us (0.905)
  Pallas kernels: 66.4 us -> 61.3 us
  local copies, waits for them, and re-layouts: 6.04 us -> 4.09 us
    pallas_call x1, Pallas kernels: 66.4 us -> 55 us  [local(): pl.pallas_call(functools.partial(entry, (nzh, nzl, ncol, block, width, fe...]
    pallas_call x0 -> x1, Pallas kernels: none -> 6.25 us  [local(): pl.pallas_call(functools.partial(finish, width + 1, features, 1.0 / (nz *...]
    pallas_call x1 -> x0, local copies, waits for them, and re-layouts: 1.65 us -> none  [local(): pl.pallas_call(functools.partial(entry, (nzh, nzl, ncol, block, width, fe...]
    unnamed x2 -> x10, local copies, waits for them, and re-layouts: 4.39 us -> 4.09 us
where the time goes in v2:
time: 66.3 us; the launch traced here: 66 us
  Pallas kernels  61.3 us (92%)
  local copies, waits for them, and re-layouts  4.09 us (6%)
    pallas_call x1, Pallas kernels, local(): pl.pallas_call(functools.partial(entry, (nzh, nzl, ncol, block, width, fe...  55 us
    pallas_call x1, Pallas kernels, local(): pl.pallas_call(functools.partial(finish, width + 1, features, 1.0 / (nz *...  6.25 us
    unnamed x10, local copies, waits for them, and re-layouts  4.09 us

profile of v2, /device:TPU:1, one launch (start us, length us, event | category | flops | bytes accessed | tf_op | source)
XLA Modules:
  0.0 66.0 jit_solution(6973145282619183538)
XLA Ops:
  0.6 0.0 copy-start.2
  0.6 0.7 %copy-done.2 = f32[16,240]{1,0:T(8,128)S(1)} copy-done((f32[16,240]{1,0:T(8,128)S(1)}, f32[16,240]{1,0:T(8,128)}, u32[]{:S(2)}) %copy-start.2) | copy-done | bytes 15384
  1.3 0.0 copy-start.3
  1.4 0.7 %copy-done.3 = f32[16,240]{1,0:T(8,128)S(1)} copy-done((f32[16,240]{1,0:T(8,128)S(1)}, f32[16,240]{1,0:T(8,128)}, u32[]{:S(2)}) %copy-start.3) | copy-done | bytes 15384
  2.1 0.0 copy-start.4
  2.1 0.7 %copy-done.4 = s32[8,2]{0,1:T(2,128)S(1)} copy-done((s32[8,2]{0,1:T(2,128)S(1)}, s32[8,2]{0,1:T(2,128)}, u32[]{:S(2)}) %copy-start.4) | copy-done | bytes 88
  2.7 55.0 %shard_map.50 = (f32[8,256,256]{2,1,0:T(8,128)S(1)}, f32[1,120,256]{2,1,0:T(8,128)S(1)}) custom-call(s32[2,8]{1,0:T(2,128)S(1)} %bitcast.3, f32[16,240]{1,0:T(8,128)S(1)} %copy-done.2, f32[16,240]{1,0:T(8,128)S(1)} %copy-done.3), custom_call_target="tpu_custom_call" | custom-call | tf_op jit(solution)/shard_map/pallas_call | solution.py:269
  57.8 0.0 copy-start
  57.8 1.3 %copy-done = f32[8,256,256]{2,1,0:T(8,128)} copy-done((f32[8,256,256]{2,1,0:T(8,128)}, f32[8,256,256]{2,1,0:T(8,128)S(1)}, u32[]{:S(2)}) %copy-start) | copy-done | bytes 2097176
  59.1 0.0 copy-start.1
  59.1 0.6 copy-done.1
  59.8 6.2 %shard_map.51 = (f32[8,256,256]{2,1,0:T(8,128)}, f32[1,120,256]{2,1,0:T(8,128)}) custom-call(s32[2,8]{1,0:T(2,128)} %bitcast.2, f32[8,256,256]{2,1,0:T(8,128)} %copy-done, f32[1,120,256]{2,1,0:T(8,128)} %copy-done.1), custom_call_target="tpu_custom_call" | custom-call | tf_op jit(solution)/shard_map/pallas_call | solution.py:296
Async XLA Ops:
  0.6 0.7 %copy-start.2 = (f32[16,240]{1,0:T(8,128)S(1)}, f32[16,240]{1,0:T(8,128)}, u32[]{:S(2)}) copy-start(f32[16,240]{1,0:T(8,128)} %refs_1_.1) | copy-start | bytes 46084
  1.3 0.7 %copy-start.3 = (f32[16,240]{1,0:T(8,128)S(1)}, f32[16,240]{1,0:T(8,128)}, u32[]{:S(2)}) copy-start(f32[16,240]{1,0:T(8,128)} %refs_2_.1) | copy-start | bytes 46084
  2.1 0.7 %copy-start.4 = (s32[8,2]{0,1:T(2,128)S(1)}, s32[8,2]{0,1:T(2,128)}, u32[]{:S(2)}) copy-start(s32[8,2]{0,1:T(2,128)} %param.5) | copy-start | bytes 196
  57.8 1.4 %copy-start = (f32[8,256,256]{2,1,0:T(8,128)}, f32[8,256,256]{2,1,0:T(8,128)S(1)}, u32[]{:S(2)}) copy-start(f32[8,256,256]{2,1,0:T(8,128)S(1)} %get-tuple-element.6.turned_ref) | copy-start | bytes 6291460
  59.1 0.6 copy-start.1

commit v3 on v2

v3 whole, which is shorter than its diff:
```python
import functools

import jax
import jax.numpy as jnp
from jax import lax
from jax.experimental import pallas as pl
from jax.experimental.pallas import tpu as pltpu
from jax.sharding import PartitionSpec as P

TW = 256
CTILES = 114
LANES = 128
GROUP = 16
LEAD = GROUP - 1
COPIES = 536
MESH = pl.DeviceIdType.MESH
NT = (((1,), (1,)), ((), ()))
NN = (((1,), (0,)), ((), ()))
HIGH = lax.Precision.HIGH


def ring_slots(nz):
    up = {d: 2 * d - 1 for d in range(1, nz // 2 + 1)}
    down = {d: 2 * d for d in range(1, (nz + 1) // 2)}
    return up, down


def tile_place(tile, width):
    column = tile * TW
    shift = lax.div(column, width)
    first = column - shift * width
    second = first + shift
    second = jnp.where(second >= width, second - width, second)
    turn = lax.rem(first + GROUP - 1, GROUP)
    wrap = lax.div(width - first + turn, GROUP)
    return turn, wrap, first - turn + LEAD, second - turn + LEAD


def feature_part(feat, plane, place):
    turn, wrap, left, right = place
    rows = lax.broadcasted_iota(jnp.int32, (GROUP, LANES), 0)

    def read(start, size):
        return feat[plane, pl.ds(start, size), :]

    head_left = jnp.where(rows >= turn, read(left, GROUP), read(left + TW, GROUP))
    tail_right = jnp.where(rows >= GROUP * wrap - GROUP + 1, read(right + TW + 2, GROUP), read(right + TW + 1, GROUP))
    head_right = jnp.where(rows >= turn, read(right, GROUP), tail_right)
    body_left = read(left + GROUP, TW - GROUP)
    body_right = [read(right + GROUP * g + jnp.where(g >= wrap, 1, 0), GROUP) for g in range(1, TW // GROUP)]
    return jnp.concatenate([head_left * head_right, body_left * jnp.concatenate(body_right, 0)], 0)


def turn_rows(turned, value, turn):
    for h in range(value.shape[1] // LANES):
        part = value[:, h * LANES : (h + 1) * LANES]
        turned[h, :TW] = part
        turned[h, TW:] = part[:GROUP]
    return jnp.concatenate([turned[h, pl.ds(turn, TW), :] for h in range(value.shape[1] // LANES)], 1)


def pair_places(map_ref, p, width):
    return [tile_place(jnp.maximum(map_ref[q, p], 0), width) for q in range(2)]


def finish(width, features, inv_snaps, map_ref, turned_ref, rhs_in_ref, gram_ref, rhs_ref, taken, given, turned, side, took, gave, rhs_sem):
    slots = taken.shape[0]
    rhs_take = pltpu.make_async_copy(rhs_in_ref, side, rhs_sem.at[0])
    rhs_give = pltpu.make_async_copy(side, rhs_ref, rhs_sem.at[1])
    rhs_take.start()

    def take(p):
        return pltpu.make_async_copy(turned_ref.at[p], taken.at[p], took.at[p])

    def give(p):
        return pltpu.make_async_copy(given.at[p], gram_ref.at[p], gave.at[p])

    for p in range(slots):
        take(p).start()

    def one(p, carry):
        take(p).wait()
        (a, *_), (b, *_) = pair_places(map_ref, p, width)
        total = pltpu.roll(turn_rows(turned, taken[p], a), lax.rem(TW - b, TW), 1)
        row_at = lax.broadcasted_iota(jnp.int32, (TW, TW), 0) + map_ref[0, p] * TW
        col_at = lax.broadcasted_iota(jnp.int32, (TW, TW), 1) + map_ref[1, p] * TW
        live = (map_ref[0, p] >= 0) & (row_at < features) & (col_at < features)
        given[p] = jnp.where(live, total * inv_snaps, 0.0)
        give(p).start()
        return carry

    lax.fori_loop(0, slots, one, 0)
    rhs_take.wait()
    rhs_give.start()
    rhs_give.wait()
    for p in range(slots):
        give(p).wait()


def turn_plane(tile):
    return jnp.concatenate([tile[:, :LANES].T, tile[:, LANES:].T], 0)


def kernel(sizes, map_ref, states_ref, derivs_ref, gram_ref, rhs_ref, bufs, sems):
    nzh, nzl, ncol, block, states, features = sizes
    nz = nzh * nzl
    far = nz // 2
    width = states + 1
    half = states // nzh
    slots = gram_ref.shape[0]
    per_core = ncol * block // LANES
    up_slot, down_slot = ring_slots(nz)
    zh, row, col = lax.axis_index("snap"), lax.axis_index("row"), lax.axis_index("col")
    core = lax.rem(row, 2)
    z = zh * nzl + lax.div(row, 2)
    inv_snaps = 1.0 / (nz * 2 * ncol * block)
    own, halves, plane_rows, column = bufs["own"], bufs["halves"], bufs["plane_rows"], bufs["column"]
    land, derivs, feat, turned = bufs["land"], bufs["derivs"], bufs["feat"], bufs["turned"]

    def device(z_to, core_to, col_to):
        return {"snap": lax.div(z_to, nzl), "row": lax.rem(z_to, nzl) * 2 + core_to, "col": col_to}

    def along_z(e):
        return device(lax.rem(z + e + nz, nz), core, col)

    def in_plane(k):
        return device(z, core, lax.rem(col + k, ncol))

    sibling = device(z, 1 - core, col)

    def copy(src, dst, kind, index, to):
        send, recv = sems[kind]
        return pltpu.make_async_remote_copy(
            src_ref=src, dst_ref=dst, send_sem=send.at[index], recv_sem=recv.at[index], device_id=to, device_id_type=MESH
        )

    def each(first, last, act):
        lax.fori_loop(first, last, lambda k, c: (act(k), c)[1], 0)

    load_states = pltpu.make_async_copy(states_ref, bufs["states"], sems["load"][0].at[0])
    load_derivs = pltpu.make_async_copy(derivs_ref, bufs["given"], sems["load"][1].at[0])
    load_states.start()
    load_derivs.start()
    barrier = pltpu.get_barrier_semaphore()

    def greet(to):
        pl.semaphore_signal(barrier, inc=1, device_id=to, device_id_type=MESH)

    greet(sibling)
    each(1, nz, lambda e: greet(along_z(e)))
    each(1, ncol, lambda k: greet(in_plane(k)))

    load_states.wait()
    load_derivs.wait()
    own[...] = jnp.ones(own.shape, jnp.float32)
    own[:, :states] = bufs["states"][...]
    for h in range(nzh):
        halves[h] = jnp.zeros((block, LANES), jnp.float32)
        halves[h, :, :half] = bufs["given"][:, h * half : (h + 1) * half]
    plane_rows[col] = own[...]
    column[0] = halves[zh]

    pl.semaphore_wait(barrier, 1 + (nz - 1) + (ncol - 1))

    def plane_copy(k):
        return copy(own, plane_rows.at[col], "plane", k, in_plane(k))

    def column_copy(e):
        slot = up_slot[e] if e in up_slot else down_slot[nz - e]
        z_to = lax.rem(z + e, nz)
        return copy(halves.at[lax.div(z_to, nzl)], column.at[slot], "column", slot, along_z(e))

    def spread_copy(k):
        return copy(column, derivs.at[0, :, col], "spread", k, in_plane(k))

    def across_copy():
        return copy(derivs.at[0], derivs.at[1], "across", 0, sibling)

    def ring_copies(d, n):
        copies = []
        for slot_of, way, takes in ((up_slot, 1, n < (per_core + 1) // 2), (down_slot, -1, n >= (per_core + 1) // 2)):
            if d < far or (d == far and takes):
                src = slot_of[d - 1] if d > 1 else 0
                dst = slot_of[d] if d < far else up_slot[far]
                copies.append(copy(land.at[src, 0, n], land.at[dst, 0, n], "ring", dst * per_core + n, along_z(way)))
        return copies

    def slots_at(d):
        return [0] if d == 0 else [s[d] for s in (up_slot, down_slot) if d in s]

    def share(slot, n):
        return copy(land.at[slot, 0, n], land.at[slot, 1, n], "share", slot * per_core + n, sibling)

    def pass_on(d, n):
        for c in ring_copies(d, n):
            c.wait_recv()
        for c in ring_copies(d + 1, n):
            c.start()
        for slot in slots_at(d):
            share(slot, n).start()

    def planes_of(d, ns):
        return [(s * 2 + c) * per_core + n for s in slots_at(d) for c in range(2) for n in ns]

    def unfold(d, ns):
        for slot in slots_at(d):
            for n in ns:
                share(slot, n).wait_recv()

        def one(m, carry):
            slot = slots_at(d)[0] + lax.div(m, 2 * len(ns))
            c, n = lax.rem(lax.div(m, len(ns)), 2), lax.rem(m, len(ns)) + ns[0]
            rows = land[slot, c, n][:width]
            plane = (slot * 2 + c) * per_core + n
            feat[plane, :LEAD] = rows[width - LEAD :]
            feat[plane, LEAD : LEAD + width] = rows
            feat[plane, LEAD + width : LEAD + 2 * width] = rows
            feat[plane, LEAD + 2 * width :] = rows[: COPIES - LEAD - 2 * width]
            return carry

        lax.fori_loop(0, len(slots_at(d)) * 2 * len(ns), one, 0)

    def tile_value(place, planes):
        return jnp.concatenate([feature_part(feat, plane, place) for plane in planes], 1)

    def gram(planes, first_time, midway=None):
        together = slots // 2

        def one(h, carry):
            if midway is not None:
                pl.when(h == 1)(midway)
            for j in range(together):
                p = h * together + j
                a, b = pair_places(map_ref, p, width)
                term = lax.dot_general(
                    tile_value(a, planes), tile_value(b, planes), NT, precision=HIGH, preferred_element_type=jnp.float32
                )
                gram_ref[p] = term if first_time else gram_ref[p] + term
            return carry

        lax.fori_loop(0, 2, one, 0)

    both = list(range(per_core))
    low, high = both[: (per_core + 1) // 2], both[(per_core + 1) // 2 :]

    def pass_all(d, ns):
        for n in ns:
            pass_on(d, n)

    each(1, ncol, lambda k: plane_copy(k).start())
    for e in range(1, nz):
        column_copy(e).start()
    each(1, ncol, lambda k: plane_copy(k).wait_recv())
    for n in both:
        land[0, 0, n] = turn_plane(plane_rows[...].reshape(per_core, LANES, 2 * LANES)[n])
        for c in ring_copies(1, n):
            c.start()
        share(0, n).start()
    for slot in range(1, nz):
        copy(halves.at[0], column.at[slot], "column", slot, sibling).wait_recv()
    derivs[0, :, col] = column[...]
    each(1, ncol, lambda k: spread_copy(k).start())

    unfold(0, both)
    gram(planes_of(0, both), True)
    pass_all(1, low)
    unfold(1, low)
    gram(planes_of(1, low), False, functools.partial(pass_all, 1, high))
    if high:
        unfold(1, high)
        gram(planes_of(1, high), False, functools.partial(pass_all, 2, low))
    else:
        pass_all(2, low)
    for d in range(2, far + 1):
        pass_all(d, high)
        if d == far:
            each(1, ncol, lambda k: spread_copy(k).wait_recv())
            across_copy().start()
        unfold(d, both)
        gram(planes_of(d, both), False, functools.partial(pass_all, d + 1, low) if d < far else None)

    across_copy().wait_recv()
    rhs_tile = lax.rem(row * ncol + col, CTILES)
    place = tile_place(rhs_tile, width)
    parts = [derivs[c, s].reshape(ncol * block, LANES) for s in range(nz) for c in range(2)]
    total = lax.dot_general(
        tile_value(place, range(nz * 2 * per_core)),
        jnp.concatenate(parts, 0),
        NN,
        precision=HIGH,
        preferred_element_type=jnp.float32,
    )
    total = turn_rows(turned, total, place[0])
    row_at = lax.broadcasted_iota(jnp.int32, total.shape, 0) + rhs_tile * TW
    total = jnp.where(row_at < features, total * inv_snaps, 0.0)
    turned_rhs = jnp.concatenate([total[:LANES].T, total[LANES:].T], 1)
    rhs_ref[0] = turned_rhs[:half]

    each(1, ncol, lambda k: plane_copy(k).wait_send())
    each(1, ncol, lambda k: spread_copy(k).wait_send())
    for e in range(1, nz):
        column_copy(e).wait_send()
    for n in both:
        for d in range(1, far + 1):
            for c in ring_copies(d, n):
                c.wait_send()
        for slot in range(nz):
            share(slot, n).wait_send()
    across_copy().wait_send()


def entry(sizes, names, kinds, *refs):
    refs, flat = refs[: -2 * len(kinds)], refs[-2 * len(kinds) :]
    refs, bufs = refs[: -len(names)], refs[-len(names) :]
    kernel(sizes, *refs, dict(zip(names, bufs)), {k: flat[2 * i : 2 * i + 2] for i, k in enumerate(kinds)})


def local(nzh, nzl, ncol, states, derivatives, tile_map):
    block, width = states.shape
    nz = nzh * nzl
    per_core = ncol * block // LANES
    features = (width + 1) * ((width + 2) // 2)
    slots = tile_map.shape[0]
    shapes = {
        "states": (block, width),
        "given": (block, width),
        "own": (block, 2 * LANES),
        "halves": (nzh, block, LANES),
        "plane_rows": (ncol, block, 2 * LANES),
        "column": (nz, block, LANES),
        "land": (nz, 2, per_core, 2 * LANES, LANES),
        "derivs": (2, nz, ncol, block, LANES),
        "feat": (nz * 2 * per_core, COPIES, LANES),
        "turned": (2, TW + GROUP, LANES),
    }
    counts = {
        "load": 1,
        "plane": ncol,
        "column": nz,
        "spread": ncol,
        "across": 1,
        "ring": nz * per_core,
        "share": nz * per_core,
    }
    out_shape = (
        jax.ShapeDtypeStruct((slots, TW, TW), jnp.float32),
        jax.ShapeDtypeStruct((1, width // nzh, TW), jnp.float32),
    )
    smem, vmem, anywhere = (pl.BlockSpec(memory_space=m) for m in (pltpu.SMEM, pltpu.VMEM, pl.ANY))
    gram_tiles, rhs = pl.pallas_call(
        functools.partial(entry, (nzh, nzl, ncol, block, width, features), tuple(shapes), tuple(counts)),
        out_shape=out_shape,
        in_specs=[smem, anywhere, anywhere],
        out_specs=[vmem, vmem],
        scratch_shapes=[pltpu.VMEM(shape, jnp.float32) for shape in shapes.values()]
        + [pltpu.SemaphoreType.DMA((count,)) for count in counts.values() for _ in range(2)],
        compiler_params=pltpu.CompilerParams(collective_id=0, has_side_effects=True, vmem_limit_bytes=60 * 2**20),
    )(tile_map.T, states, derivatives)
    gram_tiles, rhs = pl.pallas_call(
        functools.partial(finish, width + 1, features, 1.0 / (nz * 2 * ncol * block)),
        out_shape=out_shape,
        in_specs=[smem, anywhere, anywhere],
        out_specs=[anywhere, anywhere],
        scratch_shapes=[
            pltpu.VMEM((slots, TW, TW), jnp.float32),
            pltpu.VMEM((slots, TW, TW), jnp.float32),
            pltpu.VMEM((2, TW + GROUP, LANES), jnp.float32),
            pltpu.VMEM((1, width // nzh, TW), jnp.float32),
            pltpu.SemaphoreType.DMA((slots,)),
            pltpu.SemaphoreType.DMA((slots,)),
            pltpu.SemaphoreType.DMA((2,)),
        ],
        compiler_params=pltpu.CompilerParams(vmem_limit_bytes=60 * 2**20),
    )(tile_map.T, gram_tiles, rhs)
    return gram_tiles, rhs.transpose(0, 2, 1)


def solution(mesh):
    nzh, rows, ncol = mesh.shape["snap"], mesh.shape["row"], mesh.shape["col"]
    placed = P(("snap", "row", "col"), None)
    return jax.shard_map(
        functools.partial(local, nzh, rows // 2, ncol),
        mesh=mesh,
        in_specs=(placed, placed, placed),
        out_specs=(P(("snap", "row", "col"), None, None), P(("row", "col"), None, "snap")),
        check_vma=False,
    )
```

time: 66.3 us -> 59.2 us (0.89)
  local copies, waits for them, and re-layouts: 4.09 us -> 0 us
  Pallas kernels: 61.3 us -> 58.1 us
    unnamed x10 -> x0, local copies, waits for them, and re-layouts: 4.09 us -> none
    pallas_call x1, Pallas kernels: 6.25 us -> 3.89 us  [local(): pl.pallas_call(functools.partial(finish, width + 1, features, 1.0 / (nz *...]
    pallas_call x1, Pallas kernels: 55 us -> 54.2 us  [local(): pl.pallas_call(functools.partial(entry, (nzh, nzl, ncol, block, width, fe...]
where the time goes in v3:
time: 59.2 us; the launch traced here: 58.9 us
  Pallas kernels  58.1 us (98%)
  between operations  0.8 us (1%)
    pallas_call x1, Pallas kernels, local(): pl.pallas_call(functools.partial(entry, (nzh, nzl, ncol, block, width, fe...  54.2 us
    pallas_call x1, Pallas kernels, local(): pl.pallas_call(functools.partial(finish, width + 1, features, 1.0 / (nz *...  3.89 us

profile of v3, /device:TPU:1, one launch (start us, length us, event | category | flops | bytes accessed | tf_op | source)
XLA Modules:
  0.0 58.9 jit_solution(18249011804077672462)
XLA Ops:
  0.6 54.2 %shard_map.50 = (f32[8,256,256]{2,1,0:T(8,128)}, f32[1,120,256]{2,1,0:T(8,128)}) custom-call(s32[2,8]{1,0:T(2,128)} %bitcast.2, f32[16,240]{1,0:T(8,128)} %refs_1_.1, f32[16,240]{1,0:T(8,128)} %refs_2_.1), custom_call_target="tpu_custom_call" | custom-call | tf_op jit(solution)/shard_map/pallas_call | solution.py:350
  54.8 3.9 %shard_map.51 = (f32[8,256,256]{2,1,0:T(8,128)}, f32[1,120,256]{2,1,0:T(8,128)}) custom-call(s32[2,8]{1,0:T(2,128)} %bitcast.3, f32[8,256,256]{2,1,0:T(8,128)} %get-tuple-element.6.turned_ref, f32[1,120,256]{2,1,0:T(8,128)} %get-tuple-element.7.rhs_in_ref), custom_call_target="tpu_custom_call" | custom-call | tf_op jit(solution)/shard_map/pallas_call | solution.py:359

commit v4 on v3

--- a/solution.py
+++ b/solution.py
@@ -16,7 +16,6 @@
 MESH = pl.DeviceIdType.MESH
 NT = (((1,), (1,)), ((), ()))
 NN = (((1,), (0,)), ((), ()))
-HIGH = lax.Precision.HIGH
 
 
 def ring_slots(nz):
@@ -97,6 +96,20 @@
         give(p).wait()
 
 
+def split(value):
+    high = value.astype(jnp.bfloat16)
+    return high, (value - high.astype(jnp.float32)).astype(jnp.bfloat16)
+
+
+def product(left, right, dims):
+    (left_high, left_low), (right_high, right_low) = split(left), split(right)
+
+    def dot(a, b):
+        return lax.dot_general(a, b, dims, preferred_element_type=jnp.float32)
+
+    return dot(left_high, right_high) + dot(left_low, right_high) + dot(left_high, right_low)
+
+
 def turn_plane(tile):
     return jnp.concatenate([tile[:, :LANES].T, tile[:, LANES:].T], 0)
 
@@ -107,7 +120,8 @@
     far = nz // 2
     width = states + 1
     half = states // nzh
-    slots = gram_ref.shape[0]
+    gram_sum = bufs["gram"]
+    slots = gram_sum.shape[0]
     per_core = ncol * block // LANES
     up_slot, down_slot = ring_slots(nz)
     zh, row, col = lax.axis_index("snap"), lax.axis_index("row"), lax.axis_index("col")
@@ -223,7 +237,10 @@
     def tile_value(place, planes):
         return jnp.concatenate([feature_part(feat, plane, place) for plane in planes], 1)
 
-    def gram(planes, first_time, midway=None):
+    def give(p):
+        return pltpu.make_async_copy(gram_sum.at[p], gram_ref.at[p], sems["give"][0].at[p])
+
+    def gram(planes, first_time=False, last_time=False, midway=None):
         together = slots // 2
 
         def one(h, carry):
@@ -232,10 +249,10 @@
             for j in range(together):
                 p = h * together + j
                 a, b = pair_places(map_ref, p, width)
-                term = lax.dot_general(
-                    tile_value(a, planes), tile_value(b, planes), NT, precision=HIGH, preferred_element_type=jnp.float32
-                )
-                gram_ref[p] = term if first_time else gram_ref[p] + term
+                term = product(tile_value(a, planes), tile_value(b, planes), NT)
+                gram_sum[p] = term if first_time else gram_sum[p] + term
+                if last_time:
+                    give(p).start()
             return carry
 
         lax.fori_loop(0, 2, one, 0)
@@ -262,39 +279,34 @@
     each(1, ncol, lambda k: spread_copy(k).start())
 
     unfold(0, both)
-    gram(planes_of(0, both), True)
+    gram(planes_of(0, both), first_time=True)
     pass_all(1, low)
-    unfold(1, low)
-    gram(planes_of(1, low), False, functools.partial(pass_all, 1, high))
-    if high:
-        unfold(1, high)
-        gram(planes_of(1, high), False, functools.partial(pass_all, 2, low))
-    else:
-        pass_all(2, low)
-    for d in range(2, far + 1):
-        pass_all(d, high)
-        if d == far:
-            each(1, ncol, lambda k: spread_copy(k).wait_recv())
-            across_copy().start()
-        unfold(d, both)
-        gram(planes_of(d, both), False, functools.partial(pass_all, d + 1, low) if d < far else None)
+    for d in range(1, far):
+        unfold(d, low)
+        gram(planes_of(d, low), midway=functools.partial(pass_all, d, high))
+        if high:
+            unfold(d, high)
+            gram(planes_of(d, high), midway=functools.partial(pass_all, d + 1, low))
+        else:
+            pass_all(d + 1, low)
+    pass_all(far, high)
+    each(1, ncol, lambda k: spread_copy(k).wait_recv())
+    across_copy().start()
+    unfold(far, both)
+    gram(planes_of(far, both), last_time=True)
 
     across_copy().wait_recv()
     rhs_tile = lax.rem(row * ncol + col, CTILES)
     place = tile_place(rhs_tile, width)
     parts = [derivs[c, s].reshape(ncol * block, LANES) for s in range(nz) for c in range(2)]
-    total = lax.dot_general(
-        tile_value(place, range(nz * 2 * per_core)),
-        jnp.concatenate(parts, 0),
-        NN,
-        precision=HIGH,
-        preferred_element_type=jnp.float32,
-    )
+    total = product(tile_value(place, range(nz * 2 * per_core)), jnp.concatenate(parts, 0), NN)
     total = turn_rows(turned, total, place[0])
     row_at = lax.broadcasted_iota(jnp.int32, total.shape, 0) + rhs_tile * TW
     total = jnp.where(row_at < features, total * inv_snaps, 0.0)
     turned_rhs = jnp.concatenate([total[:LANES].T, total[LANES:].T], 1)
     rhs_ref[0] = turned_rhs[:half]
+
+    each(0, slots, lambda p: give(p).wait())
 
     each(1, ncol, lambda k: plane_copy(k).wait_send())
     each(1, ncol, lambda k: spread_copy(k).wait_send())
@@ -332,9 +344,11 @@
         "derivs": (2, nz, ncol, block, LANES),
         "feat": (nz * 2 * per_core, COPIES, LANES),
         "turned": (2, TW + GROUP, LANES),
+        "gram": (slots, TW, TW),
     }
     counts = {
         "load": 1,
+        "give": slots,
         "plane": ncol,
         "column": nz,
         "spread": ncol,
@@ -351,7 +365,7 @@
         functools.partial(entry, (nzh, nzl, ncol, block, width, features), tuple(shapes), tuple(counts)),
         out_shape=out_shape,
         in_specs=[smem, anywhere, anywhere],
-        out_specs=[vmem, vmem],
+        out_specs=[anywhere, vmem],
         scratch_shapes=[pltpu.VMEM(shape, jnp.float32) for shape in shapes.values()]
         + [pltpu.SemaphoreType.DMA((count,)) for count in counts.values() for _ in range(2)],
         compiler_params=pltpu.CompilerParams(collective_id=0, has_side_effects=True, vmem_limit_bytes=60 * 2**20),

time: 59.2 us -> 55.6 us (0.939)
  Pallas kernels: 58.1 us -> 54.7 us
    pallas_call x1, Pallas kernels: 54.2 us -> 50.8 us  [local(): pl.pallas_call(functools.partial(entry, (nzh, nzl, ncol, block, width, fe...]
where the time goes in v4:
time: 55.6 us; the launch traced here: 55.3 us
  Pallas kernels  54.7 us (98%)
  between operations  0.64 us (1%)
    pallas_call x1, Pallas kernels, local(): pl.pallas_call(functools.partial(entry, (nzh, nzl, ncol, block, width, fe...  50.8 us
    pallas_call x1, Pallas kernels, local(): pl.pallas_call(functools.partial(finish, width + 1, features, 1.0 / (nz *...  3.89 us

profile of v4, /device:TPU:1, one launch (start us, length us, event | category | flops | bytes accessed | tf_op | source)
XLA Modules:
  0.0 55.3 jit_solution(12675615104974156867)
XLA Ops:
  0.6 50.8 %shard_map.50 = (f32[8,256,256]{2,1,0:T(8,128)}, f32[1,120,256]{2,1,0:T(8,128)}) custom-call(s32[2,8]{1,0:T(2,128)} %bitcast.2, f32[16,240]{1,0:T(8,128)} %refs_1_.1, f32[16,240]{1,0:T(8,128)} %refs_2_.1), custom_call_target="tpu_custom_call" | custom-call | tf_op jit(solution)/shard_map/pallas_call | solution.py:364
  51.4 3.9 %shard_map.51 = (f32[8,256,256]{2,1,0:T(8,128)}, f32[1,120,256]{2,1,0:T(8,128)}) custom-call(s32[2,8]{1,0:T(2,128)} %bitcast.3, f32[8,256,256]{2,1,0:T(8,128)} %get-tuple-element.6.turned_ref, f32[1,120,256]{2,1,0:T(8,128)} %get-tuple-element.7.rhs_in_ref), custom_call_target="tpu_custom_call" | custom-call | tf_op jit(solution)/shard_map/pallas_call | solution.py:373

commit v5 on v4

--- a/solution.py
+++ b/solution.py
@@ -107,7 +107,9 @@
     def dot(a, b):
         return lax.dot_general(a, b, dims, preferred_element_type=jnp.float32)
 
-    return dot(left_high, right_high) + dot(left_low, right_high) + dot(left_high, right_low)
+    rows = left.shape[0]
+    both = dot(jnp.concatenate([left_high, left_low], 0), right_high)
+    return both[:rows] + both[rows:] + dot(left_high, right_low)
 
 
 def turn_plane(tile):
@@ -241,7 +243,7 @@
         return pltpu.make_async_copy(gram_sum.at[p], gram_ref.at[p], sems["give"][0].at[p])
 
     def gram(planes, first_time=False, last_time=False, midway=None):
-        together = slots // 2
+        together = slots // 2 if midway is not None else slots
 
         def one(h, carry):
             if midway is not None:
@@ -255,7 +257,7 @@
                     give(p).start()
             return carry
 
-        lax.fori_loop(0, 2, one, 0)
+        lax.fori_loop(0, slots // together, one, 0)
 
     both = list(range(per_core))
     low, high = both[: (per_core + 1) // 2], both[(per_core + 1) // 2 :]

time: 55.6 us -> 55.7 us (level)
  no operation moved by 1% of the time
where the time goes in v5:
time: 55.7 us; the launch traced here: 55.5 us
  Pallas kernels  54.7 us (98%)
  between operations  0.8 us (1%)
    pallas_call x1, Pallas kernels, local(): pl.pallas_call(functools.partial(entry, (nzh, nzl, ncol, block, width, fe...  50.8 us
    pallas_call x1, Pallas kernels, local(): pl.pallas_call(functools.partial(finish, width + 1, features, 1.0 / (nz *...  3.89 us

profile of v5, /device:TPU:1, one launch (start us, length us, event | category | flops | bytes accessed | tf_op | source)
XLA Modules:
  0.0 55.5 jit_solution(13551868732784843315)
XLA Ops:
  0.6 50.8 %shard_map.50 = (f32[8,256,256]{2,1,0:T(8,128)}, f32[1,120,256]{2,1,0:T(8,128)}) custom-call(s32[2,8]{1,0:T(2,128)} %bitcast.2, f32[16,240]{1,0:T(8,128)} %refs_1_.1, f32[16,240]{1,0:T(8,128)} %refs_2_.1), custom_call_target="tpu_custom_call" | custom-call | tf_op jit(solution)/shard_map/pallas_call | solution.py:366
  51.4 3.9 %shard_map.51 = (f32[8,256,256]{2,1,0:T(8,128)}, f32[1,120,256]{2,1,0:T(8,128)}) custom-call(s32[2,8]{1,0:T(2,128)} %bitcast.3, f32[8,256,256]{2,1,0:T(8,128)} %get-tuple-element.6.turned_ref, f32[1,120,256]{2,1,0:T(8,128)} %get-tuple-element.7.rhs_in_ref), custom_call_target="tpu_custom_call" | custom-call | tf_op jit(solution)/shard_map/pallas_call | solution.py:375
